TPU v7x, 32 devices: a whole 2x2x4 slice. The times are simulated.
32 devices in a mesh: heads: 4 (over y, x), seq: 8 (over z, core).
Axes of the slice: x: 2, y: 2, z: 4, core: 2. Of those that a mesh axis runs over, the one named last changes fastest.
Arguments:
- queries: bfloat16 [4096, 2048], P('seq', 'heads'), may hold values from -64 to 64
- keys: bfloat16 [4096, 512], P('seq', 'heads'), may hold values from -6 to 6
- values: bfloat16 [4096, 512], P('seq', 'heads'), may hold values from -6 to 6
- vertical: int32 [16, 16], replicated, may hold values from 0 to 63, as said below
- slash: int32 [16, 8], replicated, may hold values from 0 to 15, as said below
- out_weight: bfloat16 [2048, 4096], P('heads'), may hold values from -0.25 to 0.25
Outputs:
- layer_out: bfloat16 [4096, 4096], P('seq', 'heads')
Inputs may be any that keep to these rules, and one draw needn't show every extreme that they name: `vertical`: each row lists 16 distinct blocks; the four rows of one KV head (rows 4g to 4g+3) list 64 distinct blocks in all; at most 8 of those lie within blocks k * 8 to (k + 1) * 8 - 1 for any k, and in every draw some k reaches 8. `slash`: each row lists 8 distinct offsets, 0 among them; some row holds 15 in every draw.
All inputs are finite; a program needn't handle non-finite values.
Results may differ from a plain program's by a relative error of at most 0.0095.
Values may be sent and summed in bfloat16 or wider, within the bound.
A program may use at most 128 MiB of HBM per device.

v0:
```python
import math

import jax
import jax.numpy as jnp
from jax import lax
from jax.sharding import PartitionSpec as P

HEAD_SIZE = 128
BLOCK_TOKENS = 64


def from_behind(block, axis, distance):
    devices = range(lax.axis_size(axis))
    route = [(i - distance, i) for i in devices if i - distance in devices]
    return lax.ppermute(block, axis, route)


def attend_head(query_rows, vert_pair, context, vert_blocks, offsets, first_block):
    block_count = context.shape[1] // 3
    head_dim = query_rows.shape[1]
    score_scale = 1.0 / math.sqrt(head_dim)
    block_rows = query_rows.reshape(block_count, BLOCK_TOKENS, head_dim)
    near_pair = jax.vmap(
        lambda offset: lax.dynamic_slice_in_dim(context, 2 * block_count - offset, block_count, 1)
    )(offsets)
    score_vert = (
        jnp.einsum("abd,nkd->abnk", block_rows, vert_pair[0], preferred_element_type=jnp.float32)
        * score_scale
    )
    score_diag = (
        jnp.einsum(
            "abd,nakd->abnk", block_rows, near_pair[:, 0], preferred_element_type=jnp.float32
        )
        * score_scale
    )
    query_block = first_block + jnp.arange(block_count, dtype=jnp.int32)
    token_pos = jnp.arange(BLOCK_TOKENS)
    causal_tri = token_pos[None, :] <= token_pos[:, None]
    vert_here = vert_blocks[None, None, :, None]
    block_here = query_block[:, None, None, None]
    allow_vert = (vert_here < block_here) | (vert_here == block_here) & causal_tri[None, :, None, :]
    target = query_block[None, :] - offsets[:, None]
    listed = jnp.any(vert_blocks[:, None, None] == target[None, :, :], axis=0)
    keep = (target >= 0) & jnp.logical_not(listed)
    allow_diag = keep.T[:, None, :, None] & (
        (offsets != 0)[None, None, :, None] | causal_tri[None, :, None, :]
    )
    top_vert = jnp.max(jnp.where(allow_vert, score_vert, -jnp.inf), axis=(2, 3), keepdims=True)
    top_diag = jnp.max(jnp.where(allow_diag, score_diag, -jnp.inf), axis=(2, 3), keepdims=True)
    row_top = jnp.maximum(top_vert, top_diag)
    expo_vert = jnp.where(allow_vert, jnp.exp(score_vert - row_top), 0.0)
    expo_diag = jnp.where(allow_diag, jnp.exp(score_diag - row_top), 0.0)
    row_total = jnp.sum(expo_vert, axis=(2, 3), keepdims=True) + jnp.sum(
        expo_diag, axis=(2, 3), keepdims=True
    )
    weight_vert = (expo_vert / row_total).astype(jnp.bfloat16)
    weight_diag = (expo_diag / row_total).astype(jnp.bfloat16)
    result = jnp.einsum(
        "abnk,nkd->abd", weight_vert, vert_pair[1], preferred_element_type=jnp.float32
    )
    result = result + jnp.einsum(
        "abnk,nakd->abd", weight_diag, near_pair[:, 1], preferred_element_type=jnp.float32
    )
    return result.reshape(block_count * BLOCK_TOKENS, head_dim).astype(jnp.bfloat16)


def local(queries, keys, values, vertical, slash, out_weight):
    head_dim = HEAD_SIZE
    local_heads = queries.shape[1] // head_dim
    token_count = queries.shape[0]
    block_count = token_count // BLOCK_TOKENS
    cycle_size = lax.axis_size("seq")
    kv_group = lax.axis_index("heads")
    cycle_index = lax.axis_index("seq")
    vert_group = lax.dynamic_slice_in_dim(vertical, kv_group * local_heads, local_heads, 0)
    slash_group = lax.dynamic_slice_in_dim(slash, kv_group * local_heads, local_heads, 0)
    union_list = vert_group.reshape(-1)
    listed_count = union_list.shape[0]
    owner_dev = union_list // block_count
    within_dev = union_list % block_count
    paired = jnp.stack([keys, values]).reshape(2, block_count, BLOCK_TOKENS, head_dim)
    owned_here = owner_dev == cycle_index
    capacity = min(block_count, max(2, 2 * listed_count // cycle_size))
    positions = jnp.arange(listed_count)
    same_owner = (owner_dev[:, None] == owner_dev[None, :]) & (
        positions[None, :] < positions[:, None]
    )
    slot_index = jnp.sum(same_owner.astype(jnp.int32), axis=1)
    selector = owned_here[None, :] & (slot_index[None, :] == jnp.arange(capacity)[:, None])
    picked = jnp.sum(jnp.where(selector, within_dev[None, :], 0), axis=1)
    outgoing = paired[:, picked].reshape(2, capacity * BLOCK_TOKENS, head_dim)
    arrived = lax.all_gather(outgoing, "seq", axis=1, tiled=True)
    arrived = arrived.reshape(2, cycle_size * capacity, BLOCK_TOKENS, head_dim)
    chosen = arrived[:, owner_dev * capacity + slot_index]
    chosen = chosen.reshape(2, local_heads, vert_group.shape[1], BLOCK_TOKENS, head_dim)
    earlier = from_behind(paired, "seq", 1)
    farther = from_behind(paired, "seq", 2)
    context = jnp.concatenate([farther, earlier, paired], axis=1)
    first_block = cycle_index * block_count
    outputs = []
    for head_index in range(local_heads):
        query_rows = queries[:, head_index * head_dim : (head_index + 1) * head_dim]
        outputs.append(
            attend_head(
                query_rows,
                chosen[:, head_index],
                context,
                vert_group[head_index],
                slash_group[head_index],
                first_block,
            )
        )
    attention = jnp.concatenate(outputs, axis=1)
    term = jnp.dot(attention, out_weight, preferred_element_type=jnp.float32)
    layer_out = lax.psum_scatter(
        term.astype(jnp.bfloat16), "heads", scatter_dimension=1, tiled=True
    )
    return layer_out


def solution(mesh):
    return jax.shard_map(
        local,
        mesh=mesh,
        in_specs=(
            P("seq", "heads"),
            P("seq", "heads"),
            P("seq", "heads"),
            P(),
            P(),
            P("heads", None),
        ),
        out_specs=P("seq", "heads"),
        check_vma=False,
    )
```

profile of v0, /device:TPU:0, one launch (start us, length us, event | category | flops | bytes accessed | tf_op | source)
XLA Modules:
  0.0 141.6 jit_solution(4342512957920789759)
XLA Ops:
  6.6 1.1 pad_maximum_fusion
  7.7 4.9 %collective-permute-start = (bf16[2,8,64,128]{3,2,0,1:T(8,128)(2,1)S(1)}, bf16[2,8,64,128]{3,2,0,1:T(8,128)(2,1)S(1)}, u32[]{:S(2)}, u32[]{:S(2)}) collective-permute-start(bf16[2,8,64,128]{3,2,0,1:T(8,128)(2,1)S(1)} %pad_maximum_fusion), channel_id=1, source_target_pairs={{0,2},{1,3},{2,4},{3,5},{4,6},{5,7},{8,10},{9,11},{10,12},{11,13},... | collective-permute-start | bytes 786440 | tf_op jit(solution)/shard_map/ppermute | solution.py:15
  12.6 1.5 %collective-permute-start.1 = (bf16[2,8,64,128]{3,2,0,1:T(8,128)(2,1)S(1)}, bf16[2,8,64,128]{3,2,0,1:T(8,128)(2,1)S(1)}, u32[]{:S(2)}, u32[]{:S(2)}) collective-permute-start(bf16[2,8,64,128]{3,2,0,1:T(8,128)(2,1)S(1)} %pad_maximum_fusion), channel_id=1, source_target_pairs={{0,1},{1,2},{2,3},{3,4},{4,5},{5,6},{6,7},{8,9},{9,10},{10,11},{11... | collective-permute-start | bytes 786440 | tf_op jit(solution)/shard_map/ppermute | solution.py:15
  23.7 2.2 %gather_fusion.2 = bf16[8,2,8,64,128]{4,3,1,2,0:T(8,128)(2,1)} fusion(bf16[2,24,64,128]{3,2,0,1:T(8,128)(2,1)S(1)} %maximum_maximum_fusion, s32[8]{0:T(128)S(1)} %get-tuple-element.82), kind=kCustom, calls=%fused_computation.2 | custom fusion | bytes 4194432 | tf_op jit(solution)/shard_map/vmap()/gather | solution.py:24
  25.9 2.2 %gather_fusion.3 = bf16[8,2,8,64,128]{4,3,1,2,0:T(8,128)(2,1)} fusion(bf16[2,24,64,128]{3,2,0,1:T(8,128)(2,1)S(1)} %maximum_maximum_fusion, s32[8]{0:T(128)S(1)} %get-tuple-element.81), kind=kCustom, calls=%fused_computation.3 | custom fusion | bytes 4194432 | tf_op jit(solution)/shard_map/vmap()/gather | solution.py:24
  28.1 2.2 %gather_fusion.4 = bf16[8,2,8,64,128]{4,3,1,2,0:T(8,128)(2,1)} fusion(bf16[2,24,64,128]{3,2,0,1:T(8,128)(2,1)S(1)} %maximum_maximum_fusion, s32[8]{0:T(128)S(1)} %get-tuple-element.80), kind=kCustom, calls=%fused_computation.4 | custom fusion | bytes 4194432 | tf_op jit(solution)/shard_map/vmap()/gather | solution.py:24
  30.3 1.1 gather_fusion.5
  31.4 2.9 %fusion.96 = (bf16[8,1,8,64,128]{4,3,1,2,0:T(8,128)(2,1)}, bf16[8,1,8,64,128]{4,3,1,2,0:T(8,128)(2,1)S(1)}) fusion(bf16[8,2,8,64,128]{4,3,1,2,0:T(8,128)(2,1)} %gather_fusion.2), kind=kLoop, calls=%fused_computation.232 | loop fusion | bytes 4194304 | tf_op jit(solution)/shard_map/slice | solution.py:62
  34.3 1.1 fusion.97
  36.3 1.2 fusion.98
  37.5 1.1 fusion.99
  38.6 1.9 %fusion.16 = (f32[8,64]{1,0:T(8,128)S(1)}, f32[8,8,64,64]{3,2,1,0:T(8,128)}) fusion(pred[64,8,64]{0,2,1:T(8,128)(4,1)S(1)} %get-tuple-element.41, pred[8,8]{1,0:T(8,128)(4,1)S(1)} %copy-done.25, bf16[8,64,128,1]{2,1,3,0:T(8,128)(2,1)S(1)} %bitcast.384, bf16[8,1,8,64,128]{4,3,1,2,0:T(8,128)(2,1)S(1)} %get-tuple-element.27), kind=kOutput, calls=%fused_computation.47 | convolution fusion | flops 68156928 | bytes 2263104 | tf_op jit(solution)/shard_map/abd,nakd->abnk/dot_general | solution.py:31
  40.5 1.9 %fusion.17 = (f32[8,64]{1,0:T(8,128)S(1)}, f32[8,8,64,64]{3,2,1,0:T(8,128)}) fusion(pred[64,8,64]{0,2,1:T(8,128)(4,1)S(1)} %get-tuple-element.40, pred[8,8]{1,0:T(8,128)(4,1)S(1)} %copy-done.24, bf16[8,64,128,1]{2,1,3,0:T(8,128)(2,1)S(1)} %bitcast.382, bf16[8,1,8,64,128]{4,3,1,2,0:T(8,128)(2,1)S(1)} %get-tuple-element.29), kind=kOutput, calls=%fused_computation.48 | convolution fusion | flops 68156928 | bytes 2263104 | tf_op jit(solution)/shard_map/abd,nakd->abnk/dot_general | solution.py:31
  42.4 1.8 %fusion.18 = (f32[8,64]{1,0:T(8,128)S(1)}, f32[8,8,64,64]{3,2,1,0:T(8,128)}) fusion(pred[64,8,64]{0,2,1:T(8,128)(4,1)S(1)} %get-tuple-element.38, pred[8,8]{1,0:T(8,128)(4,1)S(1)} %copy-done.23, bf16[8,64,128,1]{2,1,3,0:T(8,128)(2,1)S(1)} %bitcast.378, bf16[8,1,8,64,128]{4,3,1,2,0:T(8,128)(2,1)S(1)} %get-tuple-element.31), kind=kOutput, calls=%fused_computation.49 | convolution fusion | flops 68156928 | bytes 2263104 | tf_op jit(solution)/shard_map/abd,nakd->abnk/dot_general | solution.py:31
  44.3 1.8 %fusion.19 = (f32[8,64]{1,0:T(8,128)S(1)}, f32[8,8,64,64]{3,2,1,0:T(8,128)}) fusion(pred[64,8,64]{0,2,1:T(8,128)(4,1)S(1)} %get-tuple-element.39, pred[8,8]{1,0:T(8,128)(4,1)S(1)} %copy-done.22, bf16[8,64,128,1]{2,1,3,0:T(8,128)(2,1)S(1)} %bitcast.380, bf16[8,1,8,64,128]{4,3,1,2,0:T(8,128)(2,1)S(1)} %get-tuple-element.32), kind=kOutput, calls=%fused_computation.50 | convolution fusion | flops 68156928 | bytes 2263104 | tf_op jit(solution)/shard_map/abd,nakd->abnk/dot_general | solution.py:31
  46.2 2.7 %gather_fusion.1 = bf16[64,2,64,128]{3,2,1,0:T(8,128)(2,1)S(1)} fusion(bf16[2,64,64,128]{3,2,1,0:T(8,128)(2,1)} %bitcast.371, s32[1024]{0:T(1024)} %pad_clamp_fusion), kind=kCustom, calls=%fused_computation.1 | custom fusion | bytes 4194560 | tf_op jit(solution)/shard_map/gather | solution.py:94
  50.7 1.2 fusion.9
  53.2 4.7 %fusion.12 = (f32[8,64]{1,0:T(8,128)S(1)}, f32[8,64]{1,0:T(8,128)S(1)}, f32[8,64]{1,0:T(8,128)S(1)}, f32[8,64]{1,0:T(8,128)S(1)}, f32[16,64,8,64]{3,1,2,0:T(8,128)S(1)}) fusion(f32[16,64,8,64]{3,1,2,0:T(8,128)S(1)} %get-tuple-element.69, f32[8,64]{1,0:T(8,128)S(1)} %max.32, pred[64,64]{0,1:T(8,128)(4,1)S(1)} %iota_compare_fusion.1, ...), kind=kOutput, calls=%fused_computation.35 | convolution fusion | flops 145225728 | bytes 15110144 | tf_op jit(solution)/shard_map/abd,nkd->abnk/dot_general | solution.py:27
  57.9 0.9 convolution_bitcast_fusion.3
  58.8 1.6 %fusion.43 = bf16[8,64,128]{2,1,0:T(8,128)(2,1)S(1)} fusion(f32[8,64,128]{2,1,0:T(8,128)S(1)} %convolution_bitcast_fusion.3, f32[16,64,8,64]{3,1,2,0:T(8,128)S(1)} %get-tuple-element.69, f32[8,64]{1,0:T(8,128)S(1)} %add.168, f32[8,64]{1,0:T(8,128)S(1)} %max.32, pred[64,64]{0,1:T(8,128)(4,1)S(1)} %iota_compare_fusion.1, pred[8,16]{0,1:T(8,128)(4,1)S(1)} %copy-done.27, ...), kind=kOutput, calls=%fused_computation.86 | convolution fusion | flops 138018816 | bytes 4870144 | tf_op jit(solution)/shard_map/abnk,nkd->abd/dot_general | solution.py:58
  60.4 0.9 fusion.29
  61.3 4.9 %fusion.13 = (f32[8,64]{1,0:T(8,128)S(1)}, f32[8,64]{1,0:T(8,128)S(1)}, f32[8,64]{1,0:T(8,128)S(1)}) fusion(f32[16,64,8,64]{3,1,2,0:T(8,128)S(1)} %get-tuple-element.72, f32[8,64]{1,0:T(8,128)S(1)} %max.33, pred[8,16]{0,1:T(8,128)(4,1)S(1)} %copy-done.20, pred[8,16]{0,1:T(8,128)(4,1)S(1)} %copy-done.21, pred[64,64]{0,1:T(8,128)(4,1)S(1)} %iota_compare_fusion.1, ...), kind=kLoop, calls=%fused_computation.36 | loop fusion | flops 9435648 | bytes 6308608 | tf_op jit(solution)/shard_map/reduce_sum | solution.py:53
  66.2 0.9 convolution_bitcast_fusion.2
  67.1 1.6 %fusion.42 = bf16[8,64,128]{2,1,0:T(8,128)(2,1)S(1)} fusion(f32[8,64,128]{2,1,0:T(8,128)S(1)} %convolution_bitcast_fusion.2, f32[16,64,8,64]{3,1,2,0:T(8,128)S(1)} %get-tuple-element.72, f32[8,64]{1,0:T(8,128)S(1)} %add.172, f32[8,64]{1,0:T(8,128)S(1)} %max.33, pred[8,16]{0,1:T(8,128)(4,1)S(1)} %copy-done.20, pred[8,16]{0,1:T(8,128)(4,1)S(1)} %copy-done.21, ...), kind=kOutput, calls=%fused_computation.85 | convolution fusion | flops 138018816 | bytes 4870144 | tf_op jit(solution)/shard_map/abnk,nkd->abd/dot_general | solution.py:58
  68.7 0.8 fusion.30
  69.9 0.9 convolution_bitcast_fusion.1
  70.9 1.6 %fusion.41 = bf16[8,64,128]{2,1,0:T(8,128)(2,1)S(1)} fusion(f32[8,64,128]{2,1,0:T(8,128)S(1)} %convolution_bitcast_fusion.1, f32[16,64,8,64]{3,1,2,0:T(8,128)S(1)} %fusion.64, f32[8,64]{1,0:T(8,128)S(1)} %add.176, f32[8,64]{1,0:T(8,128)S(1)} %max.34, pred[8,16]{0,1:T(8,128)(4,1)S(1)} %copy-done.18, pred[8,16]{0,1:T(8,128)(4,1)S(1)} %copy-done.19, ...), kind=kOutput, calls=%fused_computation.84 | convolution fusion | flops 138018816 | bytes 4870144 | tf_op jit(solution)/shard_map/abnk,nkd->abd/dot_general | solution.py:58
  72.5 0.9 fusion.31
  73.7 0.9 convolution_bitcast_fusion
  74.6 1.6 %fusion.40 = bf16[8,64,128]{2,1,0:T(8,128)(2,1)S(1)} fusion(f32[8,64,128]{2,1,0:T(8,128)S(1)} %convolution_bitcast_fusion, f32[16,64,8,64]{3,1,2,0:T(8,128)S(1)} %fusion.63, f32[8,64]{1,0:T(8,128)S(1)} %add.180, f32[8,64]{1,0:T(8,128)S(1)} %max.35, pred[8,16]{0,1:T(8,128)(4,1)S(1)} %copy-done.17, pred[8,16]{0,1:T(8,128)(4,1)S(1)} %copy-done.16, ...), kind=kOutput, calls=%fused_computation.83 | convolution fusion | flops 138018816 | bytes 4870144 | tf_op jit(solution)/shard_map/abnk,nkd->abd/dot_general | solution.py:58
  76.8 4.3 %convolution_convert_fusion = bf16[512,4096]{1,0:T(8,128)(2,1)} fusion(bf16[512,4096]{1,0:T(8,128)(2,1)S(1)} %copy-done.29, bf16[512,128]{1,0:T(8,128)(2,1)S(1)} %bitcast.389, bf16[512,128]{1,0:T(8,128)(2,1)S(1)} %bitcast.388, bf16[512,128]{1,0:T(8,128)(2,1)S(1)} %bitcast.387, bf16[512,128]{1,0:T(8,128)(2,1)S(1)} %bitcast.386), kind=kOutput, calls=%fused_computation.6 | convolution fusion | flops 2151677952 | bytes 8912896 | tf_op jit(solution)/shard_map/dot_general | solution.py:114
  81.1 53.7 %reduce-scatter.2.cloned.1.call-done = bf16[512,1024]{1,0:T(8,128)(2,1)} async-done(((bf16[512,4096]{1,0:T(8,128)(2,1)}), bf16[512,1024]{1,0:T(8,128)(2,1)}) %reduce-scatter.2.cloned.1.call-update) | async-done | bytes 1048592 | tf_op jit(solution)/shard_map/reduce_scatter | solution.py:115
  (113 shorter events, 14.8 us)
Async XLA Ops:
  6.5 7.6 %copy-start = (s32[16,16]{1,0:T(8,128)S(1)}, s32[16,16]{1,0:T(8,128)}, u32[]{:S(2)}) copy-start(s32[16,16]{1,0:T(8,128)} %param.9) | copy-start | bytes 3076
  6.5 17.1 %copy-start.13 = (bf16[512,128]{1,0:T(8,128)(2,1)S(1)}, bf16[512,128]{1,0:T(8,128)(2,1)}, u32[]{:S(2)}) copy-start(bf16[512,128]{1,0:T(8,128)(2,1)} %param.7) | copy-start | bytes 393220
  6.5 17.1 %copy-start.12 = (bf16[512,128]{1,0:T(8,128)(2,1)S(1)}, bf16[512,128]{1,0:T(8,128)(2,1)}, u32[]{:S(2)}) copy-start(bf16[512,128]{1,0:T(8,128)(2,1)} %param.8) | copy-start | bytes 393220
  6.5 16.3 %copy-start.11 = (bf16[512,512]{1,0:T(8,128)(2,1)S(1)}, bf16[512,512]{1,0:T(8,128)(2,1)}, u32[]{:S(2)}) copy-start(bf16[512,512]{1,0:T(8,128)(2,1)} %param.6) | copy-start | bytes 1572868
  6.5 39.7 %all-gather.2.cloned.1.call-start = ((), (), s32[]{:S(2)}) async-start(), calls=%async_computation.1 | async-start | bytes 2359296 | tf_op jit(solution)/shard_map/all_gather | solution.py:92
  7.7 15.9 %collective-permute-start = (bf16[2,8,64,128]{3,2,0,1:T(8,128)(2,1)S(1)}, bf16[2,8,64,128]{3,2,0,1:T(8,128)(2,1)S(1)}, u32[]{:S(2)}, u32[]{:S(2)}) collective-permute-start(bf16[2,8,64,128]{3,2,0,1:T(8,128)(2,1)S(1)} %pad_maximum_fusion), channel_id=1, source_target_pairs={{0,2},{1,3},{2,4},{3,5},{4,6},{5,7},{8,10},{9,11},{10,12},{11,13},... | collective-permute-start | bytes 786440 | tf_op jit(solution)/shard_map/ppermute | solution.py:15
  12.6 11.0 %collective-permute-start.1 = (bf16[2,8,64,128]{3,2,0,1:T(8,128)(2,1)S(1)}, bf16[2,8,64,128]{3,2,0,1:T(8,128)(2,1)S(1)}, u32[]{:S(2)}, u32[]{:S(2)}) collective-permute-start(bf16[2,8,64,128]{3,2,0,1:T(8,128)(2,1)S(1)} %pad_maximum_fusion), channel_id=1, source_target_pairs={{0,1},{1,2},{2,3},{3,4},{4,5},{5,6},{6,7},{8,9},{9,10},{10,11},{11... | collective-permute-start | bytes 786440 | tf_op jit(solution)/shard_map/ppermute | solution.py:15
  15.9 118.9 %reduce-scatter.2.cloned.1.call-start = ((), (), s32[]{:S(2)}) async-start(), calls=%async_computation.2 | async-start | bytes 5242880 | tf_op jit(solution)/shard_map/reduce_scatter | solution.py:115
  31.4 2.9 %copy-start.2 = (bf16[8,2,8,64,128]{4,3,1,2,0:T(8,128)(2,1)S(1)}, bf16[8,2,8,64,128]{4,3,1,2,0:T(8,128)(2,1)}, u32[]{:S(2)}) copy-start(bf16[8,2,8,64,128]{4,3,1,2,0:T(8,128)(2,1)} %gather_fusion.3) | copy-start | bytes 6291460
  34.3 2.0 %copy-start.1 = (bf16[8,2,8,64,128]{4,3,1,2,0:T(8,128)(2,1)S(1)}, bf16[8,2,8,64,128]{4,3,1,2,0:T(8,128)(2,1)}, u32[]{:S(2)}) copy-start(bf16[8,2,8,64,128]{4,3,1,2,0:T(8,128)(2,1)} %gather_fusion.4) | copy-start | bytes 6291460
  37.5 1.1 copy-start.14
  37.5 1.1 copy-start.25
  38.6 1.9 %copy-start.24 = (pred[8,8]{1,0:T(8,128)(4,1)S(1)}, pred[8,8]{1,0:T(8,128)(4,1)}, u32[]{:S(2)}) copy-start(pred[8,8]{1,0:T(8,128)(4,1)} %copy.48) | copy-start | bytes 196
  40.5 1.9 %copy-start.23 = (pred[8,8]{1,0:T(8,128)(4,1)S(1)}, pred[8,8]{1,0:T(8,128)(4,1)}, u32[]{:S(2)}) copy-start(pred[8,8]{1,0:T(8,128)(4,1)} %copy.53) | copy-start | bytes 196
  42.4 1.8 %copy-start.22 = (pred[8,8]{1,0:T(8,128)(4,1)S(1)}, pred[8,8]{1,0:T(8,128)(4,1)}, u32[]{:S(2)}) copy-start(pred[8,8]{1,0:T(8,128)(4,1)} %copy.58) | copy-start | bytes 196
  49.8 0.9 copy-start.15
  50.7 1.6 %copy-start.6 = (f32[8,8,64,64]{3,2,1,0:T(8,128)S(1)}, f32[8,8,64,64]{3,2,1,0:T(8,128)}, u32[]{:S(2)}) copy-start(f32[8,8,64,64]{3,2,1,0:T(8,128)} %get-tuple-element.71) | copy-start | bytes 3145732
  50.7 1.6 %copy-start.26 = (pred[8,8]{1,0:T(8,128)(4,1)S(1)}, pred[8,8]{1,0:T(8,128)(4,1)}, u32[]{:S(2)}) copy-start(pred[8,8]{1,0:T(8,128)(4,1)} %copy.43) | copy-start | bytes 196
  51.9 1.2 copy-start.16
  51.9 1.2 copy-start.17
  51.9 1.2 copy-start.18
  51.9 1.2 copy-start.19
  51.9 1.2 copy-start.20
  51.9 1.2 copy-start.21
  53.2 4.7 %copy-start.10 = (bf16[8,1,8,64,128]{4,3,1,2,0:T(8,128)(2,1)S(1)}, bf16[8,1,8,64,128]{4,3,1,2,0:T(8,128)(2,1)}, u32[]{:S(2)}) copy-start(bf16[8,1,8,64,128]{4,3,1,2,0:T(8,128)(2,1)} %get-tuple-element.26) | copy-start | bytes 3145732
  58.8 1.6 %copy-start.5 = (f32[8,8,64,64]{3,2,1,0:T(8,128)S(1)}, f32[8,8,64,64]{3,2,1,0:T(8,128)}, u32[]{:S(2)}) copy-start(f32[8,8,64,64]{3,2,1,0:T(8,128)} %get-tuple-element.74) | copy-start | bytes 3145732
  61.3 4.9 %copy-start.9 = (bf16[8,1,8,64,128]{4,3,1,2,0:T(8,128)(2,1)S(1)}, bf16[8,1,8,64,128]{4,3,1,2,0:T(8,128)(2,1)}, u32[]{:S(2)}) copy-start(bf16[8,1,8,64,128]{4,3,1,2,0:T(8,128)(2,1)} %get-tuple-element.28) | copy-start | bytes 3145732
  67.1 1.6 %copy-start.4 = (f32[8,8,64,64]{3,2,1,0:T(8,128)S(1)}, f32[8,8,64,64]{3,2,1,0:T(8,128)}, u32[]{:S(2)}) copy-start(f32[8,8,64,64]{3,2,1,0:T(8,128)} %get-tuple-element.78) | copy-start | bytes 3145732
  68.7 1.2 copy-start.8
  70.9 1.6 %copy-start.3 = (f32[8,8,64,64]{3,2,1,0:T(8,128)S(1)}, f32[8,8,64,64]{3,2,1,0:T(8,128)}, u32[]{:S(2)}) copy-start(f32[8,8,64,64]{3,2,1,0:T(8,128)} %get-tuple-element.76) | copy-start | bytes 3145732
  72.4 1.2 copy-start.7
  74.6 2.2 %copy-start.29 = (bf16[512,4096]{1,0:T(8,128)(2,1)S(1)}, bf16[512,4096]{1,0:T(8,128)(2,1)}, u32[]{:S(2)}) copy-start(bf16[512,4096]{1,0:T(8,128)(2,1)} %param.11) | copy-start | bytes 12582916
  (2 other events, 1.8 us)
Sparse Core Ops, SparseCore 0:
  16.0 30.1 all-gather.1
  81.3 53.5 reduce-scatter.1
where the time goes:
time: 142 us
  waiting for transfers between devices  53.8 us (38%)
  matrix products  29 us (20%)
  local copies, waits for them, and re-layouts  25.2 us (18%)
  between operations  13.9 us (10%)
  other arithmetic  13.2 us (9%)
  starting transfers between devices  6.49 us (5%)
    reduce_scatter x1, waiting for transfers between devices, local(): lax.psum_scatter(term.astype(jnp.bfloat16), 'heads', scatter_dimension=1,...  53.7 us
    gather x4, local copies, waits for them, and re-layouts, attend_head(): lax.dynamic_slice_in_dim(context, 2 * block_count - offset, block_count, 1)  7.66 us
    dot_general x4, matrix products, attend_head(): jnp.einsum('abd,nakd->abnk', block_rows, near_pair[:, 0], preferred_eleme...  7.49 us
    dot_general x4, matrix products, attend_head(): jnp.einsum('abd,nkd->abnk', block_rows, vert_pair[0], preferred_element_t...  7.3 us
    ppermute x2, starting transfers between devices, from_behind(): return lax.ppermute(block, axis, route)  6.42 us
    dot_general x4, matrix products, attend_head(): jnp.einsum('abnk,nkd->abd', weight_vert, vert_pair[1], preferred_element_...  6.25 us
    slice x3, local copies, waits for them, and re-layouts, attend_head(): near_pair[:, 1]  5.24 us
    reduce_sum x1, other arithmetic, attend_head(): jnp.sum(expo_vert, axis=(2, 3), keepdims=True)  4.9 us
  transfers between devices with their start and end apart: 4, of which 2 were waited for; matrix products, arithmetic and copies ran while one was open for 22% of the time, Pallas kernels for 0%

commit v1 on v0

v1 whole, which is shorter than its diff:
```python
import functools
import math

import jax
import jax.numpy as jnp
from jax import lax
from jax.experimental import pallas as pl
from jax.experimental.pallas import tpu as pltpu
from jax.sharding import PartitionSpec as P

HEAD = 128
BLOCK = 64
CHUNK = 128
REACH = 16
BAND = REACH * BLOCK + CHUNK
MASKED = -1e30
MESH = pl.DeviceIdType.MESH


def kernel(
    n_heads, n_seq, vertical, slash, q_hbm, k_hbm, v_hbm, w_hbm, out,
    q, kall, vall, kvert, vvert, wfull, abuf, bias_band, bias_vert,
    local_sem, kv_send, kv_recv, fwd_send, fwd_recv,
    w_send, w_recv, wf_send, wf_recv, a_send, a_recv,
):
    g = lax.axis_index("heads")
    s = lax.axis_index("seq")
    tokens, width = q.shape
    heads = width // HEAD
    cols = out.shape[1]
    listed = vertical.shape[1]
    vert_rows = listed * BLOCK
    n_chips = n_seq // 2
    chip, core = s // 2, s % 2
    sibling = chip * 2 + 1 - core
    first = s * (tokens // BLOCK)
    half = width // 2
    n_chunks = tokens // CHUNK
    blocks = tokens // BLOCK
    per_chunk = CHUNK // BLOCK

    barrier = pltpu.get_barrier_semaphore()
    for k in range(1, n_heads):
        pl.semaphore_signal(barrier, inc=1, device_id={"heads": (g + k) % n_heads}, device_id_type=MESH)
    pl.semaphore_signal(barrier, inc=1, device_id={"seq": sibling}, device_id_type=MESH)

    @pl.loop(1, n_chips)
    def _(d):
        pl.semaphore_signal(
            barrier, inc=1, device_id={"seq": ((chip + d) % n_chips) * 2 + core}, device_id_type=MESH
        )

    def shard(index):
        return pl.ds((index + 2) * blocks, blocks)

    def rows_of_w(group, part):
        return pl.ds(pl.multiple_of(group * width + part * half, half), half)

    own = [
        pltpu.make_async_copy(k_hbm, kall.at[shard(s)], local_sem.at[0]),
        pltpu.make_async_copy(v_hbm, vall.at[shard(s)], local_sem.at[1]),
        pltpu.make_async_copy(q_hbm, q, local_sem.at[2]),
        pltpu.make_async_copy(
            w_hbm.at[:, pl.ds(pl.multiple_of(g * cols, cols), cols)],
            wfull.at[pl.ds(pl.multiple_of(g * width, width), width)],
            local_sem.at[3],
        ),
    ]
    for copy in own:
        copy.start()
    pl.semaphore_wait(barrier, n_heads + n_chips - 1)

    sources = ((k_hbm, kall), (v_hbm, vall))

    def kv_copy(which, d, index, target):
        src, dst = sources[which]
        return pltpu.make_async_remote_copy(
            src_ref=src, dst_ref=dst.at[shard(index)],
            send_sem=kv_send.at[which, d], recv_sem=kv_recv.at[which, d],
            device_id={"seq": target}, device_id_type=MESH,
        )

    def kv_pass(which, d, index):
        dst = sources[which][1]
        return pltpu.make_async_remote_copy(
            src_ref=dst.at[shard(index)], dst_ref=dst.at[shard(index)],
            send_sem=fwd_send.at[which, d], recv_sem=fwd_recv.at[which, d],
            device_id={"seq": sibling}, device_id_type=MESH,
        )

    def w_copy(k):
        peer = (g + k) % n_heads
        return pltpu.make_async_remote_copy(
            src_ref=w_hbm.at[
                pl.ds(pl.multiple_of(core * half, half), half), pl.ds(pl.multiple_of(peer * cols, cols), cols)
            ],
            dst_ref=wfull.at[rows_of_w(g, core)],
            send_sem=w_send.at[k], recv_sem=w_recv.at[k],
            device_id={"heads": peer}, device_id_type=MESH,
        )

    def w_arrival(k):
        rows = wfull.at[rows_of_w((g + n_heads - k) % n_heads, core)]
        return pltpu.make_async_copy(rows, rows, w_recv.at[k])

    def w_pass(k, part):
        rows = wfull.at[rows_of_w((g + n_heads - k) % n_heads, part)]
        return pltpu.make_async_remote_copy(
            src_ref=rows, dst_ref=rows, send_sem=wf_send.at[k], recv_sem=wf_recv.at[k],
            device_id={"seq": sibling}, device_id_type=MESH,
        )

    @pl.loop(1, n_chips)
    def _(d):
        @pl.when(chip + d < n_chips)
        def _():
            for which in range(2):
                kv_copy(which, d, s, s + 2 * d).start()

    for k in range(1, n_heads):
        w_copy(k).start()

    empty = jnp.zeros((2 * blocks, BLOCK, HEAD), jnp.bfloat16)
    kall[pl.ds(0, 2 * blocks)] = empty
    vall[pl.ds(0, 2 * blocks)] = empty

    @pl.loop(chip + 1, n_chips)
    def _(later):
        at = pl.ds((2 * later + 2) * blocks, 2 * blocks)
        kall[at] = empty
        vall[at] = empty

    row = lax.broadcasted_iota(jnp.int32, (blocks, BAND), 0)
    place = lax.broadcasted_iota(jnp.int32, (blocks, BAND), 1) // BLOCK
    target = first + (row // per_chunk) * per_chunk - REACH + place
    offset = first + row - target
    vrow = lax.broadcasted_iota(jnp.int32, (blocks, vert_rows), 0)
    vplace = lax.broadcasted_iota(jnp.int32, (blocks, vert_rows), 1) // BLOCK

    @pl.loop(0, heads)
    def _(h):
        head = g * heads + h
        hit = jnp.zeros((blocks, BAND), jnp.int32)
        listed_block = jnp.zeros((blocks, vert_rows), jnp.int32)
        for n in range(listed):
            hit = jnp.where(target == vertical[head, n], 1, hit)
            listed_block = jnp.where(vplace == n, vertical[head, n], listed_block)
        for n in range(slash.shape[1]):
            hit = jnp.where(offset == slash[head, n], 1, hit)
        seen = (hit == 1) & (offset >= 0) & (offset < REACH) & (target >= 0)
        at = pl.ds(pl.multiple_of(h * blocks, blocks), blocks)
        bias_band[at, :] = jnp.where(seen, 0.0, MASKED)
        bias_vert[at, :] = jnp.where(listed_block <= first + vrow - REACH, 0.0, MASKED)

    own[0].wait()
    own[1].wait()
    for which in range(2):
        kv_pass(which, 0, s).start()

    @pl.loop(1, n_chips)
    def _(d):
        @pl.when(chip >= d)
        def _():
            for which in range(2):
                kv_copy(which, d, s - 2 * d, s).wait_recv()
                kv_pass(which, d, s - 2 * d).start()

    @pl.loop(0, n_chips)
    def _(d):
        @pl.when(chip >= d)
        def _():
            for which in range(2):
                kv_pass(which, d, sibling - 2 * d).wait_recv()

    own[2].wait()

    @pl.loop(0, heads * listed)
    def _(i):
        block = vertical[g * heads + i // listed, i % listed] + 2 * blocks
        kvert[i] = kall[block]
        vvert[i] = vall[block]

    scale = math.log2(math.e) / math.sqrt(HEAD)
    across = (((1,), (1,)), ((), ()))
    wide = REACH * BLOCK

    def chunk_rows(c):
        return pl.ds(pl.multiple_of(c * CHUNK, CHUNK), CHUNK)

    def group_cols(group):
        return pl.ds(pl.multiple_of(group * width, width), width)

    def a_copy(c, k):
        part = abuf.at[chunk_rows(c), group_cols(g)]
        return pltpu.make_async_remote_copy(
            src_ref=part, dst_ref=part, send_sem=a_send.at[c, k], recv_sem=a_recv.at[c, k],
            device_id={"heads": (g + k) % n_heads}, device_id_type=MESH,
        )

    def a_arrival(c, k):
        part = abuf.at[chunk_rows(c), group_cols((g + n_heads - k) % n_heads)]
        return pltpu.make_async_copy(part, part, a_recv.at[c, k])

    def spread(ref, h, c):
        rows = [
            jnp.broadcast_to(ref[pl.ds(h * blocks + c * per_chunk + a, 1), :], (BLOCK, ref.shape[1]))
            for a in range(per_chunk)
        ]
        return jnp.concatenate(rows, axis=0)

    @pl.loop(0, n_chunks)
    def _(c):
        base = first + c * per_chunk

        @pl.loop(0, heads)
        def _(h):
            col = pl.multiple_of(h * HEAD, HEAD)
            qh = q[chunk_rows(c), pl.ds(col, HEAD)]
            vrows = pl.ds(h * listed, listed)

            def flat(ref, at):
                return ref[at].reshape(at.size * BLOCK, HEAD)

            band = lax.dot_general(qh, flat(kall, pl.ds(base, REACH + per_chunk)), across, preferred_element_type=jnp.float32)
            vert = lax.dot_general(qh, flat(kvert, vrows), across, preferred_element_type=jnp.float32)
            band = band * scale + spread(bias_band, h, c)
            vert = vert * scale + spread(bias_vert, h, c)
            i = lax.broadcasted_iota(jnp.int32, (CHUNK, CHUNK), 0)
            j = lax.broadcasted_iota(jnp.int32, (CHUNK, CHUNK), 1)
            near = jnp.where(j <= i, band[:, wide:], MASKED)
            band = band[:, :wide]
            top = jnp.maximum(
                jnp.maximum(jnp.max(band, axis=1, keepdims=True), jnp.max(vert, axis=1, keepdims=True)),
                jnp.max(near, axis=1, keepdims=True),
            )
            band, vert, near = jnp.exp2(band - top), jnp.exp2(vert - top), jnp.exp2(near - top)
            total = (
                jnp.sum(band, axis=1, keepdims=True)
                + jnp.sum(vert, axis=1, keepdims=True)
                + jnp.sum(near, axis=1, keepdims=True)
            )
            mixed = jnp.dot(band.astype(jnp.bfloat16), flat(vall, pl.ds(base, REACH)), preferred_element_type=jnp.float32)
            mixed += jnp.dot(near.astype(jnp.bfloat16), flat(vall, pl.ds(base + REACH, per_chunk)), preferred_element_type=jnp.float32)
            mixed += jnp.dot(vert.astype(jnp.bfloat16), flat(vvert, vrows), preferred_element_type=jnp.float32)
            abuf[chunk_rows(c), pl.ds(pl.multiple_of(g * width + h * HEAD, HEAD), HEAD)] = (
                mixed / total
            ).astype(jnp.bfloat16)

        for k in range(1, n_heads):
            a_copy(c, k).start()

    own[3].wait()
    for k in range(1, n_heads):
        w_arrival(k).wait()
        w_pass(k, core).start()
    for k in range(1, n_heads):
        w_pass(k, 1 - core).wait_recv()

    tile = min(cols, 256)

    @pl.loop(0, n_chunks)
    def _(c):
        for k in range(1, n_heads):
            a_arrival(c, k).wait()

        @pl.loop(0, cols // tile)
        def _(t):
            at = pl.ds(pl.multiple_of(t * tile, tile), tile)
            out[chunk_rows(c), at] = jnp.dot(
                abuf[chunk_rows(c), :], wfull[:, at], preferred_element_type=jnp.float32
            ).astype(out.dtype)

    @pl.loop(0, n_chunks)
    def _(c):
        for k in range(1, n_heads):
            a_copy(c, k).wait_send()

    for k in range(1, n_heads):
        w_copy(k).wait_send()
        w_pass(k, core).wait_send()

    for which in range(2):
        kv_pass(which, 0, s).wait_send()

    @pl.loop(1, n_chips)
    def _(d):
        @pl.when(chip + d < n_chips)
        def _():
            for which in range(2):
                kv_copy(which, d, s, s + 2 * d).wait_send()

        @pl.when(chip >= d)
        def _():
            for which in range(2):
                kv_pass(which, d, s - 2 * d).wait_send()


def local(n_heads, n_seq, queries, keys, values, vertical, slash, out_weight):
    tokens, width = queries.shape
    cols = out_weight.shape[1] // n_heads
    heads = width // HEAD
    blocks = tokens // BLOCK
    n_chips = n_seq // 2
    n_chunks = tokens // CHUNK
    vert_rows = vertical.shape[1] * BLOCK
    bf16, dma = jnp.bfloat16, pltpu.SemaphoreType.DMA
    smem = pl.BlockSpec(memory_space=pltpu.SMEM)
    hbm = pl.BlockSpec(memory_space=pltpu.HBM)
    scores = heads * tokens * (BAND + vert_rows)
    return pl.pallas_call(
        functools.partial(kernel, n_heads, n_seq),
        out_shape=jax.ShapeDtypeStruct((tokens, cols), bf16),
        in_specs=[smem, smem, hbm, hbm, hbm, hbm],
        out_specs=pl.BlockSpec(memory_space=pltpu.VMEM),
        scratch_shapes=[
            pltpu.VMEM((tokens, width), bf16),
            pltpu.VMEM(((n_seq + 2) * blocks, BLOCK, HEAD), bf16),
            pltpu.VMEM(((n_seq + 2) * blocks, BLOCK, HEAD), bf16),
            pltpu.VMEM((heads * vertical.shape[1], BLOCK, HEAD), bf16),
            pltpu.VMEM((heads * vertical.shape[1], BLOCK, HEAD), bf16),
            pltpu.VMEM((n_heads * width, cols), bf16),
            pltpu.VMEM((tokens, n_heads * width), bf16),
            pltpu.VMEM((heads * blocks, BAND), jnp.float32),
            pltpu.VMEM((heads * blocks, vert_rows), jnp.float32),
            dma((4,)),
            dma((2, n_chips)), dma((2, n_chips)), dma((2, n_chips)), dma((2, n_chips)),
            dma((n_heads,)), dma((n_heads,)), dma((n_heads,)), dma((n_heads,)),
            dma((n_chunks, n_heads)), dma((n_chunks, n_heads)),
        ],
        compiler_params=pltpu.CompilerParams(
            collective_id=0, has_side_effects=True, vmem_limit_bytes=48 * 1024 * 1024
        ),
        cost_estimate=pl.CostEstimate(
            flops=4 * scores * HEAD + 2 * tokens * n_heads * width * cols,
            bytes_accessed=8 * 1024 * 1024,
            transcendentals=scores,
        ),
    )(
        vertical, slash, queries,
        keys.reshape(blocks, BLOCK, HEAD), values.reshape(blocks, BLOCK, HEAD), out_weight,
    )


def solution(mesh):
    sizes = dict(mesh.shape)
    return jax.shard_map(
        functools.partial(local, sizes["heads"], sizes["seq"]),
        mesh=mesh,
        in_specs=(P("seq", "heads"), P("seq", "heads"), P("seq", "heads"), P(), P(), P("heads", None)),
        out_specs=P("seq", "heads"),
        check_vma=False,
    )
```

time: 142 us -> 66.6 us (0.47)
  the two profiles are of different devices: /device:TPU:0 before, /device:TPU:29 now
where the time goes in v1:
time: 66.6 us; the launch traced here: 66.3 us
  Pallas kernels  58.9 us (88%)
  local copies, waits for them, and re-layouts  7.46 us (11%)
    pallas_call x1, Pallas kernels, local(): pl.pallas_call(functools.partial(kernel, n_heads, n_seq), out_shape=jax.S...  58.9 us
    unnamed x12, local copies, waits for them, and re-layouts  7.46 us

profile of v1, /device:TPU:29, one launch (start us, length us, event | category | flops | bytes accessed | tf_op | source)
XLA Modules:
  0.0 66.3 jit_solution(9110567787475509207)
XLA Ops:
  0.0 0.8 %copy.7.slash = s32[16,8]{1,0:T(8,128)S(1)} copy(s32[16,8]{0,1:T(8,128)} %param.10) | data formatting | bytes 1024 | tf_op args[4]
  0.8 0.0 copy-start
  0.8 2.2 %copy-done = bf16[512,4096]{1,0:T(8,128)(2,1)S(1)} copy-done((bf16[512,4096]{1,0:T(8,128)(2,1)S(1)}, bf16[512,4096]{1,0:T(8,128)(2,1)}, u32[]{:S(2)}) %copy-start) | copy-done | bytes 4194328
  2.9 0.0 copy-start.1
  2.9 1.0 %copy-done.1 = bf16[512,512]{1,0:T(8,128)(2,1)S(1)} copy-done((bf16[512,512]{1,0:T(8,128)(2,1)S(1)}, bf16[512,512]{1,0:T(8,128)(2,1)}, u32[]{:S(2)}) %copy-start.1) | copy-done | bytes 524312
  4.0 0.0 copy-start.2
  4.0 0.9 %copy-done.2 = bf16[512,128]{1,0:T(8,128)(2,1)S(1)} copy-done((bf16[512,128]{1,0:T(8,128)(2,1)S(1)}, bf16[512,128]{1,0:T(8,128)(2,1)}, u32[]{:S(2)}) %copy-start.2) | copy-done | bytes 131096
  4.9 0.0 copy-start.3
  4.9 0.9 %copy-done.3 = bf16[512,128]{1,0:T(8,128)(2,1)S(1)} copy-done((bf16[512,128]{1,0:T(8,128)(2,1)S(1)}, bf16[512,128]{1,0:T(8,128)(2,1)}, u32[]{:S(2)}) %copy-start.3) | copy-done | bytes 131096
  5.8 0.0 copy-start.4
  5.8 0.7 %copy-done.4 = s32[16,16]{1,0:T(8,128)S(1)} copy-done((s32[16,16]{1,0:T(8,128)S(1)}, s32[16,16]{1,0:T(8,128)}, u32[]{:S(2)}) %copy-start.4) | copy-done | bytes 1048
  6.5 58.9 %shard_map.64 = bf16[512,1024]{1,0:T(8,128)(2,1)S(1)} custom-call(s32[16,16]{1,0:T(8,128)S(1)} %copy-done.4, s32[16,8]{1,0:T(8,128)S(1)} %copy.7.slash, bf16[512,512]{1,0:T(8,128)(2,1)S(1)} %copy-done.1, bf16[8,64,128]{2,1,0:T(8,128)(2,1)S(1)} %bitcast.2, bf16[8,64,128]{2,1,0:T(8,128)(2,1)S(1)} %bitcast.3, bf16[512,4096]{1,0:T(8,128)(2,1)S(1)} %copy-done), custom_call_target="tpu_custom_call" | custom-call | flops 4429185024 | bytes 8388608 | tf_op jit(solution)/shard_map/pallas_call | solution.py:310
  65.4 1.0 %copy.9 = bf16[512,1024]{1,0:T(8,128)(2,1)} copy(bf16[512,1024]{1,0:T(8,128)(2,1)S(1)} %shard_map.64) | data formatting | bytes 2097152
Async XLA Ops:
  0.8 2.2 %copy-start = (bf16[512,4096]{1,0:T(8,128)(2,1)S(1)}, bf16[512,4096]{1,0:T(8,128)(2,1)}, u32[]{:S(2)}) copy-start(bf16[512,4096]{1,0:T(8,128)(2,1)} %w_hbm.1) | copy-start | bytes 12582916
  2.9 1.0 %copy-start.1 = (bf16[512,512]{1,0:T(8,128)(2,1)S(1)}, bf16[512,512]{1,0:T(8,128)(2,1)}, u32[]{:S(2)}) copy-start(bf16[512,512]{1,0:T(8,128)(2,1)} %q_hbm.1) | copy-start | bytes 1572868
  4.0 0.9 %copy-start.2 = (bf16[512,128]{1,0:T(8,128)(2,1)S(1)}, bf16[512,128]{1,0:T(8,128)(2,1)}, u32[]{:S(2)}) copy-start(bf16[512,128]{1,0:T(8,128)(2,1)} %param.7) | copy-start | bytes 393220
  4.9 0.9 %copy-start.3 = (bf16[512,128]{1,0:T(8,128)(2,1)S(1)}, bf16[512,128]{1,0:T(8,128)(2,1)}, u32[]{:S(2)}) copy-start(bf16[512,128]{1,0:T(8,128)(2,1)} %param.8) | copy-start | bytes 393220
  5.8 0.7 %copy-start.4 = (s32[16,16]{1,0:T(8,128)S(1)}, s32[16,16]{1,0:T(8,128)}, u32[]{:S(2)}) copy-start(s32[16,16]{1,0:T(8,128)} %vertical.1) | copy-start | bytes 3076

commit v2 on v1

--- a/solution.py
+++ b/solution.py
@@ -21,7 +21,7 @@
     n_heads, n_seq, vertical, slash, q_hbm, k_hbm, v_hbm, w_hbm, out,
     q, kall, vall, kvert, vvert, wfull, abuf, bias_band, bias_vert,
     local_sem, kv_send, kv_recv, fwd_send, fwd_recv,
-    w_send, w_recv, wf_send, wf_recv, a_send, a_recv,
+    w_send, w_recv, wf_send, wf_recv, a_send, a_recv, r_send, r_recv,
 ):
     g = lax.axis_index("heads")
     s = lax.axis_index("seq")
@@ -44,11 +44,15 @@
         pl.semaphore_signal(barrier, inc=1, device_id={"heads": (g + k) % n_heads}, device_id_type=MESH)
     pl.semaphore_signal(barrier, inc=1, device_id={"seq": sibling}, device_id_type=MESH)
 
-    @pl.loop(1, n_chips)
-    def _(d):
-        pl.semaphore_signal(
-            barrier, inc=1, device_id={"seq": ((chip + d) % n_chips) * 2 + core}, device_id_type=MESH
-        )
+    above, below = chip + 1 < n_chips, chip > 0
+
+    @pl.when(above)
+    def _():
+        pl.semaphore_signal(barrier, inc=1, device_id={"seq": s + 2}, device_id_type=MESH)
+
+    @pl.when(below)
+    def _():
+        pl.semaphore_signal(barrier, inc=1, device_id={"seq": s - 2}, device_id_type=MESH)
 
     def shard(index):
         return pl.ds((index + 2) * blocks, blocks)
@@ -68,16 +72,25 @@
     ]
     for copy in own:
         copy.start()
-    pl.semaphore_wait(barrier, n_heads + n_chips - 1)
+    neighbours = (chip + n_chips - 1) // n_chips + (2 * n_chips - 2 - chip) // n_chips
+    pl.semaphore_wait(barrier, n_heads + neighbours)
 
     sources = ((k_hbm, kall), (v_hbm, vall))
 
-    def kv_copy(which, d, index, target):
+    def kv_first(which):
         src, dst = sources[which]
         return pltpu.make_async_remote_copy(
-            src_ref=src, dst_ref=dst.at[shard(index)],
+            src_ref=src, dst_ref=dst.at[shard(s)],
+            send_sem=kv_send.at[which, 0], recv_sem=kv_recv.at[which, 0],
+            device_id={"seq": s + 2}, device_id_type=MESH,
+        )
+
+    def kv_copy(which, d, index):
+        dst = sources[which][1]
+        return pltpu.make_async_remote_copy(
+            src_ref=dst.at[shard(index)], dst_ref=dst.at[shard(index)],
             send_sem=kv_send.at[which, d], recv_sem=kv_recv.at[which, d],
-            device_id={"seq": target}, device_id_type=MESH,
+            device_id={"seq": s + 2}, device_id_type=MESH,
         )
 
     def kv_pass(which, d, index):
@@ -110,12 +123,10 @@
             device_id={"seq": sibling}, device_id_type=MESH,
         )
 
-    @pl.loop(1, n_chips)
-    def _(d):
-        @pl.when(chip + d < n_chips)
-        def _():
-            for which in range(2):
-                kv_copy(which, d, s, s + 2 * d).start()
+    @pl.when(above)
+    def _():
+        for which in range(2):
+            kv_first(which).start()
 
     for k in range(1, n_heads):
         w_copy(k).start()
@@ -145,8 +156,8 @@
         for n in range(listed):
             hit = jnp.where(target == vertical[head, n], 1, hit)
             listed_block = jnp.where(vplace == n, vertical[head, n], listed_block)
-        for n in range(slash.shape[1]):
-            hit = jnp.where(offset == slash[head, n], 1, hit)
+        for n in range(slash.shape[0]):
+            hit = jnp.where(offset == slash[n, head], 1, hit)
         seen = (hit == 1) & (offset >= 0) & (offset < REACH) & (target >= 0)
         at = pl.ds(pl.multiple_of(h * blocks, blocks), blocks)
         bias_band[at, :] = jnp.where(seen, 0.0, MASKED)
@@ -162,7 +173,12 @@
         @pl.when(chip >= d)
         def _():
             for which in range(2):
-                kv_copy(which, d, s - 2 * d, s).wait_recv()
+                kv_copy(which, d - 1, s - 2 * d).wait_recv()
+
+                @pl.when(above)
+                def _():
+                    kv_copy(which, d, s - 2 * d).start()
+
                 kv_pass(which, d, s - 2 * d).start()
 
     @pl.loop(0, n_chips)
@@ -190,16 +206,33 @@
     def group_cols(group):
         return pl.ds(pl.multiple_of(group * width, width), width)
 
+    near_groups = (g + 1 - 2 * (g % 2), (g + 2) % 4)
+    far = (near_groups[0] + 2) % 4
+
     def a_copy(c, k):
         part = abuf.at[chunk_rows(c), group_cols(g)]
         return pltpu.make_async_remote_copy(
             src_ref=part, dst_ref=part, send_sem=a_send.at[c, k], recv_sem=a_recv.at[c, k],
-            device_id={"heads": (g + k) % n_heads}, device_id_type=MESH,
+            device_id={"heads": near_groups[k]}, device_id_type=MESH,
         )
 
     def a_arrival(c, k):
-        part = abuf.at[chunk_rows(c), group_cols((g + n_heads - k) % n_heads)]
+        part = abuf.at[chunk_rows(c), group_cols(near_groups[k])]
         return pltpu.make_async_copy(part, part, a_recv.at[c, k])
+
+    def half_rows(c, k):
+        return pl.ds(pl.multiple_of(c * CHUNK + k * BLOCK, BLOCK), BLOCK)
+
+    def a_relay(c, k):
+        part = abuf.at[half_rows(c, k), group_cols(near_groups[k])]
+        return pltpu.make_async_remote_copy(
+            src_ref=part, dst_ref=part, send_sem=r_send.at[c, k], recv_sem=r_recv.at[c, k],
+            device_id={"heads": near_groups[1 - k]}, device_id_type=MESH,
+        )
+
+    def far_arrival(c, k):
+        part = abuf.at[half_rows(c, k), group_cols(far)]
+        return pltpu.make_async_copy(part, part, r_recv.at[c, k])
 
     def spread(ref, h, c):
         rows = [
@@ -246,7 +279,7 @@
                 mixed / total
             ).astype(jnp.bfloat16)
 
-        for k in range(1, n_heads):
+        for k in range(2):
             a_copy(c, k).start()
 
     own[3].wait()
@@ -258,10 +291,9 @@
 
     tile = min(cols, 256)
 
-    @pl.loop(0, n_chunks)
-    def _(c):
-        for k in range(1, n_heads):
-            a_arrival(c, k).wait()
+    def project(c):
+        for k in range(2):
+            far_arrival(c, k).wait()
 
         @pl.loop(0, cols // tile)
         def _(t):
@@ -270,10 +302,23 @@
                 abuf[chunk_rows(c), :], wfull[:, at], preferred_element_type=jnp.float32
             ).astype(out.dtype)
 
+    @pl.loop(0, n_chunks + 1)
+    def _(c):
+        @pl.when(c < n_chunks)
+        def _():
+            for k in range(2):
+                a_arrival(c, k).wait()
+                a_relay(c, k).start()
+
+        @pl.when(c > 0)
+        def _():
+            project(c - 1)
+
     @pl.loop(0, n_chunks)
     def _(c):
-        for k in range(1, n_heads):
+        for k in range(2):
             a_copy(c, k).wait_send()
+            a_relay(c, k).wait_send()
 
     for k in range(1, n_heads):
         w_copy(k).wait_send()
@@ -282,17 +327,21 @@
     for which in range(2):
         kv_pass(which, 0, s).wait_send()
 
+    @pl.when(above)
+    def _():
+        for which in range(2):
+            kv_first(which).wait_send()
+
     @pl.loop(1, n_chips)
     def _(d):
-        @pl.when(chip + d < n_chips)
-        def _():
-            for which in range(2):
-                kv_copy(which, d, s, s + 2 * d).wait_send()
-
         @pl.when(chip >= d)
         def _():
             for which in range(2):
                 kv_pass(which, d, s - 2 * d).wait_send()
+
+                @pl.when(above)
+                def _():
+                    kv_copy(which, d, s - 2 * d).wait_send()
 
 
 def local(n_heads, n_seq, queries, keys, values, vertical, slash, out_weight):
@@ -325,10 +374,10 @@
             dma((4,)),
             dma((2, n_chips)), dma((2, n_chips)), dma((2, n_chips)), dma((2, n_chips)),
             dma((n_heads,)), dma((n_heads,)), dma((n_heads,)), dma((n_heads,)),
-            dma((n_chunks, n_heads)), dma((n_chunks, n_heads)),
+            dma((n_chunks, 2)), dma((n_chunks, 2)), dma((n_chunks, 2)), dma((n_chunks, 2)),
         ],
         compiler_params=pltpu.CompilerParams(
-            collective_id=0, has_side_effects=True, vmem_limit_bytes=48 * 1024 * 1024
+            collective_id=0, has_side_effects=True, vmem_limit_bytes=60 * 1024 * 1024
         ),
         cost_estimate=pl.CostEstimate(
             flops=4 * scores * HEAD + 2 * tokens * n_heads * width * cols,
@@ -336,7 +385,7 @@
             transcendentals=scores,
         ),
     )(
-        vertical, slash, queries,
+        vertical, slash.T, queries,
         keys.reshape(blocks, BLOCK, HEAD), values.reshape(blocks, BLOCK, HEAD), out_weight,
     )
 

time: 66.6 us -> 54.5 us (0.82)
  the two profiles are of different devices: /device:TPU:29 before, /device:TPU:0 now
where the time goes in v2:
time: 54.5 us; the launch traced here: 54.3 us
  Pallas kernels  52 us (95%)
  local copies, waits for them, and re-layouts  2.26 us (4%)
    pallas_call x1, Pallas kernels, local(): pl.pallas_call(functools.partial(kernel, n_heads, n_seq), out_shape=jax.S...  52 us
    unnamed x1, local copies, waits for them, and re-layouts  2.26 us

profile of v2, /device:TPU:0, one launch (start us, length us, event | category | flops | bytes accessed | tf_op | source)
XLA Modules:
  0.0 54.3 jit_solution(1413279220401644624)
XLA Ops:
  0.0 52.0 %shard_map.64 = bf16[512,1024]{1,0:T(8,128)(2,1)} custom-call(s32[16,16]{1,0:T(8,128)} %vertical.1, s32[8,16]{1,0:T(8,128)} %bitcast.5, bf16[512,512]{1,0:T(8,128)(2,1)} %q_hbm.1, bf16[8,64,128]{2,1,0:T(8,128)(2,1)} %bitcast.3, bf16[8,64,128]{2,1,0:T(8,128)(2,1)} %bitcast.4, bf16[512,4096]{1,0:T(8,128)(2,1)} %w_hbm.1), custom_call_target="tpu_custom_call" | custom-call | flops 4429185024 | bytes 8388608 | tf_op jit(solution)/shard_map/pallas_call | solution.py:359
  52.0 2.3 %copy.8 = bf16[512,1024]{1,0:T(8,128)(2,1)} copy(bf16[512,1024]{1,0:T(8,128)(2,1)} %shard_map.64) | data formatting | bytes 2097152

commit v3 on v2

--- a/solution.py
+++ b/solution.py
@@ -245,7 +245,7 @@
     def _(c):
         base = first + c * per_chunk
 
-        @pl.loop(0, heads)
+        @pl.loop(0, heads, unroll=2)
         def _(h):
             col = pl.multiple_of(h * HEAD, HEAD)
             qh = q[chunk_rows(c), pl.ds(col, HEAD)]
@@ -282,13 +282,6 @@
         for k in range(2):
             a_copy(c, k).start()
 
-    own[3].wait()
-    for k in range(1, n_heads):
-        w_arrival(k).wait()
-        w_pass(k, core).start()
-    for k in range(1, n_heads):
-        w_pass(k, 1 - core).wait_recv()
-
     tile = min(cols, 256)
 
     def project(c):
@@ -309,6 +302,15 @@
             for k in range(2):
                 a_arrival(c, k).wait()
                 a_relay(c, k).start()
+
+        @pl.when(c == 1)
+        def _():
+            own[3].wait()
+            for k in range(1, n_heads):
+                w_arrival(k).wait()
+                w_pass(k, core).start()
+            for k in range(1, n_heads):
+                w_pass(k, 1 - core).wait_recv()
 
         @pl.when(c > 0)
         def _():

time: 54.5 us -> 54.6 us (level)
  no operation moved by 1% of the time
where the time goes in v3:
time: 54.6 us; the launch traced here: 54.3 us
  Pallas kernels  52 us (95%)
  local copies, waits for them, and re-layouts  2.26 us (4%)
    pallas_call x1, Pallas kernels, local(): pl.pallas_call(functools.partial(kernel, n_heads, n_seq), out_shape=jax.S...  52 us
    unnamed x1, local copies, waits for them, and re-layouts  2.26 us

profile of v3, /device:TPU:0, one launch (start us, length us, event | category | flops | bytes accessed | tf_op | source)
XLA Modules:
  0.0 54.3 jit_solution(2928572661766032910)
XLA Ops:
  0.0 52.0 %shard_map.64 = bf16[512,1024]{1,0:T(8,128)(2,1)} custom-call(s32[16,16]{1,0:T(8,128)} %vertical.1, s32[8,16]{1,0:T(8,128)} %bitcast.5, bf16[512,512]{1,0:T(8,128)(2,1)} %q_hbm.1, bf16[8,64,128]{2,1,0:T(8,128)(2,1)} %bitcast.3, bf16[8,64,128]{2,1,0:T(8,128)(2,1)} %bitcast.4, bf16[512,4096]{1,0:T(8,128)(2,1)} %w_hbm.1), custom_call_target="tpu_custom_call" | custom-call | flops 4429185024 | bytes 8388608 | tf_op jit(solution)/shard_map/pallas_call | solution.py:361
  52.1 2.3 %copy.8 = bf16[512,1024]{1,0:T(8,128)(2,1)} copy(bf16[512,1024]{1,0:T(8,128)(2,1)} %shard_map.64) | data formatting | bytes 2097152
